TPU v7x, 32 devices: a whole 2x2x4 slice. The times are simulated.
32 devices in a mesh: dp: 8 (over y, x, core), expert: 4 (over z).
Axes of the slice: x: 2, y: 2, z: 4, core: 2. Of those that a mesh axis runs over, the one named last changes fastest.
Arguments:
- tokens: bfloat16 [1024, 3584], P('dp', 'expert'), may hold values from -6 to 6
- gate_weight: bfloat16 [4, 1536, 3584], P('expert', 'dp'), may hold values from -0.09375 to 0.09375
- up_weight: bfloat16 [4, 1536, 3584], P('expert', 'dp'), may hold values from -0.09375 to 0.09375
- down_weight: bfloat16 [4, 1536, 3584], P('expert', 'dp'), may hold values from -0.15625 to 0.15625
- slot_tokens: int32 [4, 8], P(None, 'dp'), may hold values from 0 to 127
- slot_weights: float32 [4, 8], P(None, 'dp'), may hold values from 0.2 to 1
- out_grad: bfloat16 [1024, 3584], P('dp', 'expert'), may hold values from -6 to 6
Outputs:
- token_grad: bfloat16 [1024, 3584], P('dp', 'expert')
- gate_grad: bfloat16 [4, 1536, 3584], P('expert', 'dp')
- up_grad: bfloat16 [4, 1536, 3584], P('expert', 'dp')
- down_grad: bfloat16 [4, 1536, 3584], P('expert', 'dp')
Inputs may be any that keep to these rules, and one draw needn't show every extreme that they name: `slot_tokens`: slot c of an expert names a token of data index c // 1 by its row among that index's 128 tokens.
All inputs are finite; a program needn't handle non-finite values.
Results may differ from a plain program's by a relative error of at most 0.0057.
Values may be sent and summed in bfloat16 or wider, within the bound.
A program may use at most 64 MiB of HBM per device.

v0:
```python
import jax
import jax.numpy as jnp
from jax import lax
from jax.sharding import PartitionSpec as P


def body(tokens, gate_weight, up_weight, down_weight, slot_tokens, slot_weights, out_grad):
    picked_rows = tokens[slot_tokens]
    scaled_rows = (slot_weights[:, :, None] * out_grad[slot_tokens].astype(jnp.float32)).astype(
        jnp.bfloat16
    )
    mine_inputs, mine_grads = (
        lax.all_to_all(picked_rows, "expert", split_axis=0, concat_axis=2, tiled=True),
        lax.all_to_all(scaled_rows, "expert", split_axis=0, concat_axis=2, tiled=True),
    )
    slot_inputs = lax.all_gather(mine_inputs, "dp", axis=1, tiled=True)
    gate_pre = jnp.einsum(
        "ecd,efd->ecf", slot_inputs, gate_weight, preferred_element_type=jnp.float32
    )
    up_pre = jnp.einsum("ecd,efd->ecf", slot_inputs, up_weight, preferred_element_type=jnp.float32)
    sigmoid_gate = jax.nn.sigmoid(gate_pre)
    activated = gate_pre * sigmoid_gate
    hidden = (activated * up_pre).astype(jnp.bfloat16)
    slot_grad = lax.all_gather(mine_grads, "dp", axis=1, tiled=True)
    hidden_grad = jnp.einsum(
        "ecd,efd->ecf", slot_grad, down_weight, preferred_element_type=jnp.float32
    )
    gate_back = (
        hidden_grad * up_pre * sigmoid_gate * (1.0 + gate_pre * (1.0 - sigmoid_gate))
    ).astype(jnp.bfloat16)
    up_back = (hidden_grad * activated).astype(jnp.bfloat16)
    down_grad = jnp.einsum(
        "ecf,ecd->efd", hidden, slot_grad, preferred_element_type=jnp.float32
    ).astype(jnp.bfloat16)
    gate_grad = jnp.einsum(
        "ecf,ecd->efd", gate_back, slot_inputs, preferred_element_type=jnp.float32
    ).astype(jnp.bfloat16)
    up_grad = jnp.einsum(
        "ecf,ecd->efd", up_back, slot_inputs, preferred_element_type=jnp.float32
    ).astype(jnp.bfloat16)
    input_part = jnp.einsum(
        "ecf,efd->ecd", gate_back, gate_weight, preferred_element_type=jnp.float32
    )
    input_part = input_part + jnp.einsum(
        "ecf,efd->ecd", up_back, up_weight, preferred_element_type=jnp.float32
    )
    grad_rows = lax.psum_scatter(input_part, "dp", scatter_dimension=1, tiled=True)
    grad_back = lax.all_to_all(grad_rows, "expert", split_axis=2, concat_axis=0, tiled=True)
    flat_rows = slot_tokens.reshape(-1)
    width = tokens.shape[1]
    scaled_grad = (slot_weights[:, :, None] * grad_back).reshape(-1, width)
    token_grad = out_grad.astype(jnp.float32).at[flat_rows].add(scaled_grad).astype(jnp.bfloat16)
    return (token_grad, gate_grad, up_grad, down_grad)


def solution(mesh):
    in_specs = (
        P("dp", "expert"),
        P("expert", "dp", None),
        P("expert", "dp", None),
        P("expert", "dp", None),
        P(None, "dp"),
        P(None, "dp"),
        P("dp", "expert"),
    )
    out_specs = (
        P("dp", "expert"),
        P("expert", "dp", None),
        P("expert", "dp", None),
        P("expert", "dp", None),
    )
    return jax.shard_map(body, mesh=mesh, in_specs=in_specs, out_specs=out_specs, check_vma=False)
```

profile of v0, /device:TPU:0, one launch (start us, length us, event | category | flops | bytes accessed | tf_op | source)
XLA Modules:
  0.0 188.4 jit_solution(1760155660482255435)
XLA Ops:
  7.2 0.8 fusion.27
  8.0 1.5 gather_fusion.1
  11.4 6.3 %all-to-all-start.1 = ((bf16[4,2,448]{2,1,0:T(2,128)(2,1)}), bf16[4,2,448]{2,1,0:T(2,128)(2,1)S(1)}, u32[]{:S(2)}, u32[]{:S(2)}) async-start(bf16[4,2,448]{2,1,0:T(2,128)(2,1)} %reshape.169), calls=%async_computation.1 | async-start | bytes 16384 | tf_op jit(solution)/shard_map/all_to_all | solution.py:13
  17.7 1.5 gather_fusion
  19.3 0.7 fusion.21
  20.0 1.7 convert_element_type.58
  23.1 1.2 dynamic-slice
  24.3 5.1 %all-to-all-start = ((bf16[4,2,448]{2,1,0:T(2,128)(2,1)}), bf16[4,2,448]{2,1,0:T(2,128)(2,1)S(1)}, u32[]{:S(2)}, u32[]{:S(2)}) async-start(bf16[4,2,448]{2,1,0:T(2,128)(2,1)} %reshape.171), calls=%async_computation | async-start | bytes 16384 | tf_op jit(solution)/shard_map/all_to_all | solution.py:14
  29.5 9.2 %all_gather.7 = bf16[1,8,3584]{2,0,1:T(2,128)(2,1)S(1)} all-gather(bf16[1,1,3584]{2,0,1:T(2,128)(2,1)S(1)} %bitcast.63), channel_id=1, replica_groups=mesh['dp'=8,'expert'=4] {'dp'}, dimensions={1}, use_global_device_ids=true | all-gather | bytes 64512 | tf_op jit(solution)/shard_map/all_gather | solution.py:16
  39.8 9.4 %all_gather.6 = bf16[1,8,3584]{2,0,1:T(2,128)(2,1)S(1)} all-gather(bf16[1,1,3584]{2,0,1:T(2,128)(2,1)S(1)} %bitcast.64), channel_id=1, replica_groups=mesh['dp'=8,'expert'=4] {'dp'}, dimensions={1}, use_global_device_ids=true | all-gather | bytes 64512 | tf_op jit(solution)/shard_map/all_gather | solution.py:24
  49.2 1.7 fusion.2
  51.6 1.0 fusion.3
  52.5 1.6 fusion
  54.2 50.5 %all-reduce.3.cloned.1.call-done = f32[1,8,3584]{2,1,0:T(8,128)} async-done(((f32[1,8,3584]{2,1,0:T(8,128)}), f32[1,8,3584]{2,1,0:T(8,128)}) %all-reduce.3.cloned.1.call-update) | async-done | bytes 114704
  104.7 1.6 constant_dynamic-slice_fusion
  106.3 2.0 %copy.20 = f32[1,1,3584]{1,0,2:T(1,128)S(1)} copy(f32[1,1,3584]{2,1,0:T(1,128)S(1)} %constant_dynamic-slice_fusion) | data formatting | bytes 28672 | tf_op jit(solution)/shard_map/reduce_scatter | solution.py:47
  108.9 27.4 %reduce.4 = f32[3584]{0:T(1024)S(1)} reduce(f32[3584,1,1]{2,1,0:T(1,128)S(1)} %bitcast.62, f32[]{:T(128)} %broadcast.62), dimensions={1,2}, to_apply=%bitcast.51.reduce_sub_computation | reduce | bytes 28676
  136.9 4.6 %all-to-all-start.2 = ((f32[4,1,896]{2,1,0:T(1,128)}), f32[4,1,896]{2,1,0:T(1,128)S(1)}, u32[]{:S(2)}, u32[]{:S(2)}) async-start(f32[4,1,896]{2,1,0:T(1,128)} %reshape.173), calls=%async_computation.2 | async-start | bytes 28672 | tf_op jit(solution)/shard_map/all_to_all | solution.py:48
  141.5 1.6 fusion.1
  143.1 4.0 %all-to-all-done.2 = f32[4,1,896]{2,1,0:T(1,128)S(1)} async-done(((f32[4,1,896]{2,1,0:T(1,128)}), f32[4,1,896]{2,1,0:T(1,128)S(1)}, u32[]{:S(2)}, u32[]{:S(2)}) %all-to-all-start.2) | async-done | bytes 14368 | tf_op jit(solution)/shard_map/all_to_all | solution.py:48
  147.8 2.8 %reshape.174 = f32[3584,1,1]{2,1,0:T(1,128)S(1)} reshape(f32[4,896]{1,0:T(4,128)S(1)} %reduce.5) | data formatting | bytes 28672
  150.6 26.7 %bitcast_reduce_fusion = f32[3584]{0:T(1024)S(1)} fusion(f32[3584,1,1]{2,1,0:T(1,128)S(1)} %reshape.174), kind=kLoop, calls=%fused_computation.43 | loop fusion | bytes 28672 | tf_op jit(solution)/shard_map/all_to_all | solution.py:48
  177.4 2.4 %scatter_custom_fusion = f32[128,896]{1,0:T(8,128)} fusion(f32[128,896]{1,0:T(8,128)} %convert_element_type.58, s32[4]{0:T(128)S(1)} %fusion.27, f32[4,896]{1,0:T(4,128)S(1)} %all_to_all.32, f32[4]{0:T(128)S(1)} %bitcast.67), kind=kCustom, calls=%fused_computation.30 | custom fusion | flops 7168 | bytes 473600 | tf_op jit(solution)/shard_map/scatter-add | solution.py:52
  179.8 1.7 convert_element_type.63
  (29 shorter events, 7.0 us)
Async XLA Ops:
  7.2 31.6 %copy-start = (bf16[1,192,3584]{2,1,0:T(8,128)(2,1)S(1)}, bf16[1,192,3584]{2,1,0:T(8,128)(2,1)}, u32[]{:S(2)}) copy-start(bf16[1,192,3584]{2,1,0:T(8,128)(2,1)} %param.8) | copy-start | bytes 4128772
  7.2 32.0 %copy-start.1 = (bf16[1,192,3584]{2,1,0:T(8,128)(2,1)S(1)}, bf16[1,192,3584]{2,1,0:T(8,128)(2,1)}, u32[]{:S(2)}) copy-start(bf16[1,192,3584]{2,1,0:T(8,128)(2,1)} %param.9) | copy-start | bytes 4128772
  11.4 12.9 %all-to-all-start.1 = ((bf16[4,2,448]{2,1,0:T(2,128)(2,1)}), bf16[4,2,448]{2,1,0:T(2,128)(2,1)S(1)}, u32[]{:S(2)}, u32[]{:S(2)}) async-start(bf16[4,2,448]{2,1,0:T(2,128)(2,1)} %reshape.169), calls=%async_computation.1 | async-start | bytes 16384 | tf_op jit(solution)/shard_map/all_to_all | solution.py:13
  24.3 15.3 %all-to-all-start = ((bf16[4,2,448]{2,1,0:T(2,128)(2,1)}), bf16[4,2,448]{2,1,0:T(2,128)(2,1)S(1)}, u32[]{:S(2)}, u32[]{:S(2)}) async-start(bf16[4,2,448]{2,1,0:T(2,128)(2,1)} %reshape.171), calls=%async_computation | async-start | bytes 16384 | tf_op jit(solution)/shard_map/all_to_all | solution.py:14
  29.4 75.3 %all-reduce.3.cloned.1.call-start = ((), (), s32[]{:S(2)}) async-start(), calls=%async_computation.3 | async-start | bytes 229376
  39.8 11.0 %copy-start.2 = (bf16[1,192,3584]{2,1,0:T(8,128)(2,1)S(1)}, bf16[1,192,3584]{2,1,0:T(8,128)(2,1)}, u32[]{:S(2)}) copy-start(bf16[1,192,3584]{2,1,0:T(8,128)(2,1)} %param.10) | copy-start | bytes 4128772
  136.9 10.2 %all-to-all-start.2 = ((f32[4,1,896]{2,1,0:T(1,128)}), f32[4,1,896]{2,1,0:T(1,128)S(1)}, u32[]{:S(2)}, u32[]{:S(2)}) async-start(f32[4,1,896]{2,1,0:T(1,128)} %reshape.173), calls=%async_computation.2 | async-start | bytes 28672 | tf_op jit(solution)/shard_map/all_to_all | solution.py:48
  150.6 26.7 %copy-start.3 = (f32[4,1]{0,1:T(1,128)S(1)}, f32[4,1]{0,1:T(1,128)}, u32[]{:S(2)}) copy-start(f32[4,1]{0,1:T(1,128)} %param.12) | copy-start | bytes 52
Sparse Core Ops, SparseCore 0:
  52.7 52.0 all-reduce.2
where the time goes:
time: 189 us; the launch traced here: 188 us
  waiting for transfers between devices  54.5 us (29%)
  local copies, waits for them, and re-layouts  40.7 us (22%)
  other arithmetic  36.9 us (20%)
  blocking collectives  18.6 us (10%)
  starting transfers between devices  16 us (8%)
  between operations  14.1 us (7%)
  matrix products  7.54 us (4%)
    unnamed x2, waiting for transfers between devices  50.5 us
    unnamed x1, other arithmetic  27.4 us
    all_to_all x2, local copies, waits for them, and re-layouts, body(): lax.all_to_all(grad_rows, 'expert', split_axis=2, concat_axis=0, tiled=True)  26.7 us
    all_gather x1, blocking collectives, body(): slot_grad = lax.all_gather(mine_grads, 'dp', axis=1, tiled=True)  9.35 us
    all_gather x1, blocking collectives, body(): slot_inputs = lax.all_gather(mine_inputs, 'dp', axis=1, tiled=True)  9.23 us
    unnamed x18, local copies, waits for them, and re-layouts  8.38 us
    all_to_all x1, starting transfers between devices, body(): lax.all_to_all(picked_rows, 'expert', split_axis=0, concat_axis=2, tiled=...  6.32 us
    all_to_all x1, starting transfers between devices, body(): lax.all_to_all(scaled_rows, 'expert', split_axis=0, concat_axis=2, tiled=...  5.09 us
  transfers between devices with their start and end apart: 4, of which 2 were waited for; matrix products, arithmetic and copies ran while one was open for 6% of the time, Pallas kernels for 0%

commit v1 on v0

v1 whole, which is shorter than its diff:
```python
import functools

import jax
import jax.numpy as jnp
from jax import lax
from jax.experimental import pallas as pl
from jax.experimental.pallas import tpu as pltpu
from jax.sharding import PartitionSpec as P

MESH = pl.DeviceIdType.MESH
LANES = 128
F32 = jnp.float32
BF16 = jnp.bfloat16


def up_to(value, unit):
    return -(-value // unit) * unit


def each(count, body):
    if count <= 16:
        for i in range(count):
            body(i)
    else:
        lax.fori_loop(0, count, lambda i, carry: (body(i), carry)[1], 0)


def across(a, b):
    return lax.dot_general(a, b, (((1,), (1,)), ((), ())), preferred_element_type=F32)


def exchange_kernel(
    rows, experts, tokens, grads, gate_w, up_w, down_w, slots, weights,
    inputs_out, cotangents_out, backs_out, returned,
    tokens_v, grads_v, weights_v, stage, held, spread, sums, parts, total,
    load_sem, weight_sem, s1, r1, s2, r2, s3, r3, s4, r4,
):
    row, col = lax.axis_index("dp"), lax.axis_index("expert")
    width = tokens.shape[1]
    pieces = width // LANES
    pad16 = stage.shape[1]
    pad8 = returned.shape[1]

    loads = [
        pltpu.make_async_copy(tokens, tokens_v, load_sem.at[0]),
        pltpu.make_async_copy(grads, grads_v, load_sem.at[1]),
    ]
    weight_loads = [
        pltpu.make_async_copy(ref.at[0], weights_v.at[i], weight_sem.at[i])
        for i, ref in enumerate((gate_w, up_w, down_w))
    ]
    for load in loads:
        load.start()

    def other_row(i):
        return lax.rem(row + i + 1, rows)

    def other_col(i):
        return lax.rem(col + i + 1, experts)

    barrier = pltpu.get_barrier_semaphore()
    each(experts - 1, lambda i: pl.semaphore_signal(
        barrier, inc=1, device_id=(row, other_col(i)), device_id_type=MESH))
    each(rows - 1, lambda i: pl.semaphore_signal(
        barrier, inc=1, device_id=(other_row(i), col), device_id_type=MESH))
    for load in weight_loads:
        load.start()

    hot = (
        lax.broadcasted_iota(jnp.int32, (experts, tokens.shape[0]), 1) == slots[...]
    ).astype(F32).astype(BF16)
    loads[0].wait()
    picked = jnp.dot(hot, tokens_v[...], preferred_element_type=F32)
    loads[1].wait()
    scaled = weights[...] * jnp.dot(hot, grads_v[...], preferred_element_type=F32)
    block = [picked[:, j * LANES:(j + 1) * LANES][:, None] for j in range(pieces)]
    block += [scaled[:, j * LANES:(j + 1) * LANES][:, None] for j in range(pieces)]
    if pad16 > 2 * pieces:
        block.append(jnp.zeros((experts, pad16 - 2 * pieces, LANES), F32))
    stage[...] = jnp.concatenate(block, axis=1).astype(BF16)
    mine = pl.ds(pl.multiple_of(col * pad16, pad16), pad16)
    held[row, mine] = stage[col]
    pl.semaphore_wait(barrier, rows + experts - 2)

    def first(to, source):
        at = pl.ds(pl.multiple_of(source * pad16, pad16), pad16)
        return pltpu.make_async_remote_copy(
            src_ref=stage.at[to], dst_ref=held.at[row, at],
            send_sem=s1.at[to], recv_sem=r1.at[source],
            device_id=(row, to), device_id_type=MESH)

    each(experts - 1, lambda i: first(other_col(i), col).start())
    each(experts - 1, lambda i: first(col, other_col(i)).wait_recv())

    def second(to, source):
        return pltpu.make_async_remote_copy(
            src_ref=held.at[source], dst_ref=held.at[source],
            send_sem=s2.at[to], recv_sem=r2.at[source],
            device_id=(to, col), device_id_type=MESH)

    each(rows - 1, lambda i: second(other_row(i), row).start())

    def widen(source):
        size = experts * pad16
        spread[pl.ds(pl.multiple_of(source * size, size), size)] = held[source].astype(F32)

    widen(row)

    def arrive(i):
        source = other_row(i)
        second(row, source).wait_recv()
        widen(source)

    each(rows - 1, arrive)

    def whole_rows(base):
        return jnp.concatenate([
            spread[pl.ds(z * pad16 + base + j, rows, stride=experts * pad16), :]
            for z in range(experts) for j in range(pieces)
        ], axis=1).astype(BF16)

    inputs = whole_rows(0)
    cotangents = whole_rows(pieces)
    inputs_out[...] = inputs
    cotangents_out[...] = cotangents

    weight_loads[0].wait()
    gate_pre = across(inputs, weights_v[0])
    weight_loads[1].wait()
    up_pre = across(inputs, weights_v[1])
    weight_loads[2].wait()
    hidden_grad = across(cotangents, weights_v[2])
    sigmoid = jax.nn.sigmoid(gate_pre)
    activated = gate_pre * sigmoid
    hidden = (activated * up_pre).astype(BF16)
    gate_back = (
        hidden_grad * up_pre * sigmoid * (1.0 + gate_pre * (1.0 - sigmoid))
    ).astype(BF16)
    up_back = (hidden_grad * activated).astype(BF16)
    part = jnp.dot(gate_back, weights_v[0], preferred_element_type=F32)
    part += jnp.dot(up_back, weights_v[1], preferred_element_type=F32)
    for z in range(experts):
        for j in range(pieces):
            at = (z * pieces + j) * LANES
            parts[pl.ds(z * pad8 + j, rows, stride=experts * pad8), :] = part[:, at:at + LANES]
    slab = experts * pad8

    def third(to, source):
        return pltpu.make_async_remote_copy(
            src_ref=parts.at[pl.ds(pl.multiple_of(to * slab, slab), slab)],
            dst_ref=sums.at[source],
            send_sem=s3.at[to], recv_sem=r3.at[source],
            device_id=(to, col), device_id_type=MESH)

    each(rows - 1, lambda i: third(other_row(i), row).start())
    for i, value in enumerate((gate_back, up_back, hidden)):
        backs_out[i] = value
    total[...] = parts[pl.ds(pl.multiple_of(row * slab, slab), slab)]

    def gather_sum(i):
        source = other_row(i)
        third(row, source).wait_recv()
        total[...] += sums[source]

    each(rows - 1, gather_sum)

    def fourth(to, source):
        return pltpu.make_async_remote_copy(
            src_ref=total.at[pl.ds(pl.multiple_of(to * pad8, pad8), pad8)],
            dst_ref=returned.at[source],
            send_sem=s4.at[to], recv_sem=r4.at[source],
            device_id=(row, to), device_id_type=MESH)

    each(experts - 1, lambda i: fourth(other_col(i), col).start())
    returned[col] = total[pl.ds(pl.multiple_of(col * pad8, pad8), pad8)]

    each(experts - 1, lambda i: first(other_col(i), col).wait_send())
    each(rows - 1, lambda i: second(other_row(i), row).wait_send())
    each(rows - 1, lambda i: third(other_row(i), row).wait_send())
    each(experts - 1, lambda i: fourth(col, other_col(i)).wait_recv())
    each(experts - 1, lambda i: fourth(other_col(i), col).wait_send())


def exchange(mesh, tokens, gate_w, up_w, down_w, slots, weights, grads):
    rows, experts = mesh.shape["dp"], mesh.shape["expert"]
    width = tokens.shape[1]
    units, features = gate_w.shape[1:]
    pieces = width // LANES
    pad16, pad8 = up_to(2 * pieces, 16), up_to(pieces, 8)
    dma = pltpu.SemaphoreType.DMA
    hbm = pl.BlockSpec(memory_space=pl.ANY)
    vmem = pl.BlockSpec(memory_space=pltpu.VMEM)
    return pl.pallas_call(
        functools.partial(exchange_kernel, rows, experts),
        out_shape=(
            jax.ShapeDtypeStruct((rows, features), BF16),
            jax.ShapeDtypeStruct((rows, features), BF16),
            jax.ShapeDtypeStruct((3, rows, units), BF16),
            jax.ShapeDtypeStruct((experts, pad8, LANES), F32),
        ),
        in_specs=[hbm] * 5 + [vmem] * 2,
        out_specs=(vmem,) * 4,
        scratch_shapes=[
            pltpu.VMEM(tokens.shape, BF16),
            pltpu.VMEM(grads.shape, BF16),
            pltpu.VMEM((3, units, features), BF16),
            pltpu.VMEM((experts, pad16, LANES), BF16),
            pltpu.VMEM((rows, experts * pad16, LANES), BF16),
            pltpu.VMEM((rows * experts * pad16, LANES), F32),
            pltpu.VMEM((rows, experts * pad8, LANES), F32),
            pltpu.VMEM((rows * experts * pad8, LANES), F32),
            pltpu.VMEM((experts * pad8, LANES), F32),
            dma((2,)), dma((3,)),
            dma((experts,)), dma((experts,)), dma((rows,)), dma((rows,)),
            dma((rows,)), dma((rows,)), dma((experts,)), dma((experts,)),
        ],
        compiler_params=pltpu.CompilerParams(
            collective_id=0, has_side_effects=True, vmem_limit_bytes=44 << 20),
        name="exchange",
    )(tokens, grads, gate_w, up_w, down_w, slots, weights)


def finish_kernel(
    inputs, cotangents, backs, returned, grads, slots, weights,
    token_out, gate_out, up_out, down_out,
    wide, token_v, sems, token_sem,
):
    count, units, features = wide.shape
    experts = returned.shape[0]
    width = token_v.shape[1]
    chunk = 64 if units % 64 == 0 else units
    copies = []
    for i, out in enumerate((gate_out, up_out, down_out)):
        back = backs[i].astype(F32).T.astype(BF16)
        other = cotangents if i == 2 else inputs
        for k in range(units // chunk):
            at = pl.ds(k * chunk, chunk)
            wide[i, at] = jnp.dot(
                back[k * chunk:(k + 1) * chunk], other[...], preferred_element_type=F32
            ).astype(BF16)
            copy = pltpu.make_async_copy(
                wide.at[i, at], out.at[0, at], sems.at[i * (units // chunk) + k])
            copy.start()
            copies.append(copy)
    place = lax.broadcasted_iota(jnp.int32, (token_v.shape[0], LANES), 0)
    masks = [place == slots[e, 0] for e in range(experts)]
    for j in range(width // LANES):
        at = pl.ds(j * LANES, LANES)
        value = grads[:, at].astype(F32)
        for e in range(experts):
            line = weights[e, 0] * returned[e, pl.ds(j, 1), :]
            value += jnp.where(masks[e], line, 0.0)
        token_v[:, at] = value.astype(BF16)
    copy = pltpu.make_async_copy(token_v, token_out, token_sem)
    copy.start()
    copies.append(copy)
    for copy in copies:
        copy.wait()


def finish(inputs, cotangents, backs, returned, grads, slots, weights, like):
    units, features = like.shape[1:]
    hbm = pl.BlockSpec(memory_space=pl.ANY)
    vmem = pl.BlockSpec(memory_space=pltpu.VMEM)
    smem = pl.BlockSpec(memory_space=pltpu.SMEM)
    steps = 3 * (units // 64 if units % 64 == 0 else 1)
    wide = jax.ShapeDtypeStruct(like.shape, BF16)
    return pl.pallas_call(
        finish_kernel,
        out_shape=(jax.ShapeDtypeStruct(grads.shape, BF16), wide, wide, wide),
        in_specs=[vmem] * 5 + [smem] * 2,
        out_specs=(hbm,) * 4,
        scratch_shapes=[
            pltpu.VMEM((3, units, features), BF16),
            pltpu.VMEM(grads.shape, BF16),
            pltpu.SemaphoreType.DMA((steps,)),
            pltpu.SemaphoreType.DMA,
        ],
        compiler_params=pltpu.CompilerParams(vmem_limit_bytes=32 << 20),
        name="finish",
    )(inputs, cotangents, backs, returned, grads, slots, weights)


def solution(mesh):
    def body(tokens, gate_weight, up_weight, down_weight, slot_tokens, slot_weights, out_grad):
        inputs, cotangents, backs, returned = exchange(
            mesh, tokens, gate_weight, up_weight, down_weight, slot_tokens, slot_weights, out_grad)
        return finish(
            inputs, cotangents, backs, returned, out_grad, slot_tokens, slot_weights, gate_weight)

    split = P("dp", "expert")
    wide = P("expert", "dp", None)
    slot = P(None, "dp")
    return jax.shard_map(
        body, mesh=mesh,
        in_specs=(split, wide, wide, wide, slot, slot, split),
        out_specs=(split, wide, wide, wide),
        check_vma=False)
```

time: 189 us -> 35.2 us (0.19)
  waiting for transfers between devices: 54.5 us -> 0 us
  other arithmetic: 36.9 us -> 0 us
  local copies, waits for them, and re-layouts: 40.7 us -> 7.37 us
  Pallas kernels: 0 us -> 26.9 us
  blocking collectives: 18.6 us -> 0 us
  starting transfers between devices: 16 us -> 0 us
  between operations: 14.1 us -> 0.64 us
  matrix products: 7.54 us -> 0 us
    unnamed x2 -> x0, waiting for transfers between devices: 50.5 us -> none
    unnamed x1 -> x0, other arithmetic: 27.4 us -> none
    pallas_call x0 -> x2, Pallas kernels: none -> 26.9 us  [the longest x1 23.9 us: exchange(): pl.pallas_call(functools.partial(exchange_kernel, rows, experts), out_sha...]
    all_to_all x2 -> x0, local copies, waits for them, and re-layouts: 26.7 us -> none  [body(): lax.all_to_all(grad_rows, 'expert', split_axis=2, concat_axis=0, tiled=True)]
    all_gather x2 -> x0, blocking collectives: 18.6 us -> none  [the longest x1 9.35 us: body(): slot_grad = lax.all_gather(mine_grads, 'dp', axis=1, tiled=True)]
    all_to_all x3 -> x0, starting transfers between devices: 16 us -> none  [the longest x1 6.32 us: body(): lax.all_to_all(picked_rows, 'expert', split_axis=0, concat_axis=2, tiled=...]
    dot_general x8 -> x0, matrix products: 7.54 us -> none  [the longest x1 1.66 us: body(): jnp.einsum('ecf,ecd->efd', hidden, slot_grad, preferred_element_type=jnp....]
    convert_element_type x4 -> x0, other arithmetic: 4.86 us -> none  [the longest x2 3.47 us: body(): out_grad.astype(jnp.float32).at[flat_rows].add(scaled_grad)]
  transfers between devices with their start and end apart: 4 -> 0, of which waited for: 2 -> 0; matrix products, arithmetic and copies ran while one was open for 6% -> 0% of each run, Pallas kernels for 0% -> 0%
where the time goes in v1:
time: 35.2 us; the launch traced here: 34.9 us
  Pallas kernels  26.9 us (76%)
  local copies, waits for them, and re-layouts  7.37 us (21%)
  between operations  0.64 us (2%)
    pallas_call x1, Pallas kernels, exchange(): pl.pallas_call(functools.partial(exchange_kernel, rows, experts), out_sha...  23.9 us
    unnamed x12, local copies, waits for them, and re-layouts  7.37 us
    pallas_call x1, Pallas kernels, finish(): pl.pallas_call(finish_kernel, out_shape=(jax.ShapeDtypeStruct(grads.shape...  3.05 us

profile of v1, /device:TPU:0, one launch (start us, length us, event | category | flops | bytes accessed | tf_op | source)
XLA Modules:
  0.0 34.9 jit_solution(8709527031538636086)
XLA Ops:
  0.6 0.7 %copy.11.slots = s32[4,1]{1,0:T(4,128)S(1)} copy(s32[4,1]{0,1:T(1,128)} %param.11) | data formatting | bytes 32 | tf_op args[4]
  1.4 0.7 %copy.12.weights = f32[4,1]{1,0:T(4,128)S(1)} copy(f32[4,1]{0,1:T(1,128)} %param.12) | data formatting | bytes 32 | tf_op args[5]
  2.1 0.0 copy-start
  2.1 1.3 %copy-done = bf16[1,192,3584]{2,1,0:T(8,128)(2,1)S(1)} copy-done((bf16[1,192,3584]{2,1,0:T(8,128)(2,1)S(1)}, bf16[1,192,3584]{2,1,0:T(8,128)(2,1)}, u32[]{:S(2)}) %copy-start) | copy-done | bytes 1376280
  3.5 0.0 copy-start.1
  3.5 1.3 %copy-done.1 = bf16[1,192,3584]{2,1,0:T(8,128)(2,1)S(1)} copy-done((bf16[1,192,3584]{2,1,0:T(8,128)(2,1)S(1)}, bf16[1,192,3584]{2,1,0:T(8,128)(2,1)}, u32[]{:S(2)}) %copy-start.1) | copy-done | bytes 1376280
  4.8 0.0 copy-start.2
  4.8 1.3 %copy-done.2 = bf16[1,192,3584]{2,1,0:T(8,128)(2,1)S(1)} copy-done((bf16[1,192,3584]{2,1,0:T(8,128)(2,1)S(1)}, bf16[1,192,3584]{2,1,0:T(8,128)(2,1)}, u32[]{:S(2)}) %copy-start.2) | copy-done | bytes 1376280
  6.1 0.0 copy-start.3
  6.1 0.9 %copy-done.3 = bf16[128,896]{1,0:T(8,128)(2,1)S(1)} copy-done((bf16[128,896]{1,0:T(8,128)(2,1)S(1)}, bf16[128,896]{1,0:T(8,128)(2,1)}, u32[]{:S(2)}) %copy-start.3) | copy-done | bytes 229400
  7.1 0.0 copy-start.4
  7.1 0.9 %copy-done.4 = bf16[128,896]{1,0:T(8,128)(2,1)S(1)} copy-done((bf16[128,896]{1,0:T(8,128)(2,1)S(1)}, bf16[128,896]{1,0:T(8,128)(2,1)}, u32[]{:S(2)}) %copy-start.4) | copy-done | bytes 229400
  8.0 23.9 %exchange.1 = (bf16[8,3584]{1,0:T(8,128)(2,1)S(1)}, bf16[8,3584]{1,0:T(8,128)(2,1)S(1)}, bf16[3,8,192]{2,1,0:T(8,128)(2,1)S(1)}, f32[4,8,128]{2,1,0:T(8,128)S(1)}) custom-call(bf16[128,896]{1,0:T(8,128)(2,1)S(1)} %copy-done.4, bf16[128,896]{1,0:T(8,128)(2,1)S(1)} %copy-done.3, bf16[1,192,3584]{2,1,0:T(8,128)(2,1)S(1)} %copy-done, ...), custom_call_target="tpu_custom_call" | custom-call | tf_op jit(solution)/shard_map/exchange/pallas_call | solution.py:193
  31.9 3.0 %finish.1 = (bf16[128,896]{1,0:T(8,128)(2,1)}, bf16[1,192,3584]{2,1,0:T(8,128)(2,1)}, bf16[1,192,3584]{2,1,0:T(8,128)(2,1)}, bf16[1,192,3584]{2,1,0:T(8,128)(2,1)}) custom-call(bf16[8,3584]{1,0:T(8,128)(2,1)S(1)} %get-tuple-element.8.inputs, bf16[8,3584]{1,0:T(8,128)(2,1)S(1)} %get-tuple-element.9.cotangents, ...), custom_call_target="tpu_custom_call" | custom-call | tf_op jit(solution)/shard_map/finish/pallas_call | solution.py:268
Async XLA Ops:
  2.1 1.3 %copy-start = (bf16[1,192,3584]{2,1,0:T(8,128)(2,1)S(1)}, bf16[1,192,3584]{2,1,0:T(8,128)(2,1)}, u32[]{:S(2)}) copy-start(bf16[1,192,3584]{2,1,0:T(8,128)(2,1)} %gate_w.1) | copy-start | bytes 4128772
  3.5 1.3 %copy-start.1 = (bf16[1,192,3584]{2,1,0:T(8,128)(2,1)S(1)}, bf16[1,192,3584]{2,1,0:T(8,128)(2,1)}, u32[]{:S(2)}) copy-start(bf16[1,192,3584]{2,1,0:T(8,128)(2,1)} %up_w.1) | copy-start | bytes 4128772
  4.8 1.3 %copy-start.2 = (bf16[1,192,3584]{2,1,0:T(8,128)(2,1)S(1)}, bf16[1,192,3584]{2,1,0:T(8,128)(2,1)}, u32[]{:S(2)}) copy-start(bf16[1,192,3584]{2,1,0:T(8,128)(2,1)} %down_w.1) | copy-start | bytes 4128772
  6.1 0.9 %copy-start.3 = (bf16[128,896]{1,0:T(8,128)(2,1)S(1)}, bf16[128,896]{1,0:T(8,128)(2,1)}, u32[]{:S(2)}) copy-start(bf16[128,896]{1,0:T(8,128)(2,1)} %grads.3) | copy-start | bytes 688132
  7.1 0.9 %copy-start.4 = (bf16[128,896]{1,0:T(8,128)(2,1)S(1)}, bf16[128,896]{1,0:T(8,128)(2,1)}, u32[]{:S(2)}) copy-start(bf16[128,896]{1,0:T(8,128)(2,1)} %tokens.1) | copy-start | bytes 688132

commit v2 on v1

v2 whole, which is shorter than its diff:
```python
import functools

import jax
import jax.numpy as jnp
from jax import lax
from jax.experimental import pallas as pl
from jax.experimental.pallas import tpu as pltpu
from jax.sharding import PartitionSpec as P

MESH = pl.DeviceIdType.MESH
LANES = 128
F32 = jnp.float32
BF16 = jnp.bfloat16


def up_to(value, unit):
    return -(-value // unit) * unit


def each(count, body):
    if count <= 32:
        for i in range(count):
            body(i)
    else:
        lax.fori_loop(0, count, lambda i, carry: (body(i), carry)[1], 0)


def total_of(count, term, zero):
    if count <= 32:
        return sum((term(i) for i in range(1, count)), term(0))
    return lax.fori_loop(0, count, lambda i, value: value + term(i), zero)


def across(a, b):
    return lax.dot_general(a, b, (((1,), (1,)), ((), ())), preferred_element_type=F32)


def exchange_kernel(
    rows, experts, tokens, grads, gate_w, up_w, down_w, slots, weights,
    inputs_out, cotangents_out, backs_out, returned,
    tokens_v, grads_v, weights_v, stage, held, spread, sums, parts,
    load_sem, weight_sem, s1, r1, s2, r2,
):
    row, col = lax.axis_index("dp"), lax.axis_index("expert")
    width = tokens.shape[1]
    pieces = width // LANES
    pad16 = stage.shape[1]
    pad8 = returned.shape[1]

    loads = [
        pltpu.make_async_copy(source, target, load_sem.at[i])
        for i, (source, target) in enumerate((
            (tokens, tokens_v), (grads, grads_v)))
    ]
    weight_loads = [
        pltpu.make_async_copy(ref.at[0], weights_v.at[i], weight_sem.at[i])
        for i, ref in enumerate((gate_w, up_w, down_w))
    ]
    for load in loads:
        load.start()

    count = rows * experts
    me = row * experts + col

    def other(i):
        at = lax.rem(me + i + 1, count)
        return at, at // experts, lax.rem(at, experts)

    barrier = pltpu.get_barrier_semaphore()

    def greet(i):
        _, to_row, to_col = other(i)
        pl.semaphore_signal(barrier, inc=1, device_id=(to_row, to_col), device_id_type=MESH)

    each(count - 1, greet)
    for load in weight_loads:
        load.start()

    def column(line, kind, lanes):
        at = lax.broadcasted_iota(jnp.int32, (experts, lanes), 0)
        value = jnp.zeros((experts, lanes), kind)
        for e in range(experts):
            value = jnp.where(at == e, line[0, e], value)
        return value

    slot = column(slots, jnp.int32, tokens.shape[0])
    scale = column(weights, F32, width)
    hot = (
        lax.broadcasted_iota(jnp.int32, (experts, tokens.shape[0]), 1) == slot
    ).astype(F32).astype(BF16)
    loads[0].wait()
    picked = jnp.dot(hot, tokens_v[...], preferred_element_type=F32)
    loads[1].wait()
    scaled = scale * jnp.dot(hot, grads_v[...], preferred_element_type=F32)
    block = [picked[:, j * LANES:(j + 1) * LANES][:, None] for j in range(pieces)]
    block += [scaled[:, j * LANES:(j + 1) * LANES][:, None] for j in range(pieces)]
    if pad16 > 2 * pieces:
        block.append(jnp.zeros((experts, pad16 - 2 * pieces, LANES), F32))
    stage[...] = jnp.concatenate(block, axis=1).astype(BF16)
    mine = pl.ds(pl.multiple_of(col * pad16, pad16), pad16)
    held[row, mine] = stage[col]
    pl.semaphore_wait(barrier, count - 1)

    def direct(to, to_row, to_col, source, source_row, source_col):
        at = pl.ds(pl.multiple_of(source_col * pad16, pad16), pad16)
        return pltpu.make_async_remote_copy(
            src_ref=stage.at[to_col], dst_ref=held.at[source_row, at],
            send_sem=s1.at[to], recv_sem=r1.at[source],
            device_id=(to_row, to_col), device_id_type=MESH)

    each(count - 1, lambda i: direct(*other(i), me, row, col).start())

    def widen(source):
        size = experts * pad16
        spread[pl.ds(pl.multiple_of(source * size, size), size)] = held[source].astype(F32)

    each(count - 1, lambda i: direct(me, row, col, *other(i)).wait_recv())
    each(rows, widen)

    def whole_rows(base):
        return jnp.concatenate([
            spread[pl.ds(z * pad16 + base + j, rows, stride=experts * pad16), :]
            for z in range(experts) for j in range(pieces)
        ], axis=1).astype(BF16)

    inputs = whole_rows(0)
    cotangents = whole_rows(pieces)
    inputs_out[...] = inputs
    cotangents_out[...] = cotangents

    weight_loads[0].wait()
    gate_pre = across(inputs, weights_v[0])
    weight_loads[1].wait()
    up_pre = across(inputs, weights_v[1])
    weight_loads[2].wait()
    hidden_grad = across(cotangents, weights_v[2])
    sigmoid = jax.nn.sigmoid(gate_pre)
    activated = gate_pre * sigmoid
    hidden = (activated * up_pre).astype(BF16)
    gate_back = (
        hidden_grad * up_pre * sigmoid * (1.0 + gate_pre * (1.0 - sigmoid))
    ).astype(BF16)
    up_back = (hidden_grad * activated).astype(BF16)
    part = jnp.dot(gate_back, weights_v[0], preferred_element_type=F32)
    part += jnp.dot(up_back, weights_v[1], preferred_element_type=F32)
    for z in range(experts):
        for j in range(pieces):
            at = (z * pieces + j) * LANES
            parts[pl.ds(z * pad8 + j, rows, stride=experts * pad8), :] = part[:, at:at + LANES]

    def straight(to, to_row, to_col, source):
        at = pl.ds(pl.multiple_of(to * pad8, pad8), pad8)
        return pltpu.make_async_remote_copy(
            src_ref=parts.at[at], dst_ref=sums.at[source],
            send_sem=s2.at[to], recv_sem=r2.at[source],
            device_id=(to_row, to_col), device_id_type=MESH)

    each(count - 1, lambda i: straight(*other(i), me).start())
    for i, value in enumerate((gate_back, up_back, hidden)):
        backs_out[i] = value
    sums[me] = parts[pl.ds(pl.multiple_of(me * pad8, pad8), pad8)]
    each(count - 1, lambda i: straight(me, row, col, other(i)[0]).wait_recv())
    for e in range(experts):
        returned[e] = total_of(
            rows, lambda d, e=e: sums[d * experts + e], jnp.zeros((pad8, LANES), F32))

    each(count - 1, lambda i: direct(*other(i), me, row, col).wait_send())
    each(count - 1, lambda i: straight(*other(i), me).wait_send())


def exchange(mesh, tokens, gate_w, up_w, down_w, slots, weights, grads):
    rows, experts = mesh.shape["dp"], mesh.shape["expert"]
    width = tokens.shape[1]
    units, features = gate_w.shape[1:]
    pieces = width // LANES
    pad16, pad8 = up_to(2 * pieces, 16), up_to(pieces, 8)
    dma = pltpu.SemaphoreType.DMA
    hbm = pl.BlockSpec(memory_space=pltpu.HBM)
    vmem = pl.BlockSpec(memory_space=pltpu.VMEM)
    return pl.pallas_call(
        functools.partial(exchange_kernel, rows, experts),
        out_shape=(
            jax.ShapeDtypeStruct((rows, features), BF16),
            jax.ShapeDtypeStruct((rows, features), BF16),
            jax.ShapeDtypeStruct((3, rows, units), BF16),
            jax.ShapeDtypeStruct((experts, pad8, LANES), F32),
        ),
        in_specs=[hbm] * 5 + [pl.BlockSpec(memory_space=pltpu.SMEM)] * 2,
        out_specs=(vmem,) * 4,
        scratch_shapes=[
            pltpu.VMEM(tokens.shape, BF16),
            pltpu.VMEM(grads.shape, BF16),
            pltpu.VMEM((3, units, features), BF16),
            pltpu.VMEM((experts, pad16, LANES), BF16),
            pltpu.VMEM((rows, experts * pad16, LANES), BF16),
            pltpu.VMEM((rows * experts * pad16, LANES), F32),
            pltpu.VMEM((rows * experts, pad8, LANES), F32),
            pltpu.VMEM((rows * experts * pad8, LANES), F32),
            dma((2,)), dma((3,)),
            *[dma((rows * experts,))] * 4,
        ],
        compiler_params=pltpu.CompilerParams(
            collective_id=0, has_side_effects=True, vmem_limit_bytes=55000 << 10),
        name="exchange",
    )(tokens, grads, gate_w, up_w, down_w, slots, weights)


def finish_kernel(
    inputs, cotangents, backs, returned, grads, slots, weights,
    token_out, gate_out, up_out, down_out,
    wide, token_v, sems, token_sem,
):
    _, units, features = wide.shape
    experts = returned.shape[0]
    width = token_v.shape[1]
    chunk = 64 if units % 64 == 0 else units
    copies = []
    for i, out in enumerate((gate_out, up_out, down_out)):
        back = backs[i].astype(F32).T.astype(BF16)
        other = cotangents if i == 2 else inputs
        for k in range(units // chunk):
            at = pl.ds(k * chunk, chunk)
            wide[i, at] = jnp.dot(
                back[k * chunk:(k + 1) * chunk], other[...], preferred_element_type=F32
            ).astype(BF16)
            copy = pltpu.make_async_copy(
                wide.at[i, at], out.at[0, at], sems.at[i * (units // chunk) + k])
            copy.start()
            copies.append(copy)
    place = lax.broadcasted_iota(jnp.int32, (token_v.shape[0], LANES), 0)
    masks = [place == slots[0, e] for e in range(experts)]
    for j in range(width // LANES):
        at = pl.ds(j * LANES, LANES)
        value = grads[:, at].astype(F32)
        for e in range(experts):
            line = weights[0, e] * returned[e, pl.ds(j, 1), :]
            value += jnp.where(masks[e], line, 0.0)
        token_v[:, at] = value.astype(BF16)
    copy = pltpu.make_async_copy(token_v, token_out, token_sem)
    copy.start()
    copies.append(copy)
    for copy in copies:
        copy.wait()


def finish(inputs, cotangents, backs, returned, grads, slots, weights, like):
    units, features = like.shape[1:]
    hbm = pl.BlockSpec(memory_space=pl.ANY)
    vmem = pl.BlockSpec(memory_space=pltpu.VMEM)
    smem = pl.BlockSpec(memory_space=pltpu.SMEM)
    steps = 3 * (units // 64 if units % 64 == 0 else 1)
    wide = jax.ShapeDtypeStruct(like.shape, BF16)
    return pl.pallas_call(
        finish_kernel,
        out_shape=(jax.ShapeDtypeStruct(grads.shape, BF16), wide, wide, wide),
        in_specs=[vmem] * 5 + [smem] * 2,
        out_specs=(hbm,) * 4,
        scratch_shapes=[
            pltpu.VMEM((3, units, features), BF16),
            pltpu.VMEM(grads.shape, BF16),
            pltpu.SemaphoreType.DMA((steps,)),
            pltpu.SemaphoreType.DMA,
        ],
        compiler_params=pltpu.CompilerParams(vmem_limit_bytes=32 << 20),
        name="finish",
    )(inputs, cotangents, backs, returned, grads, slots, weights)


def solution(mesh):
    def body(tokens, gate_weight, up_weight, down_weight, slot_tokens, slot_weights, out_grad):
        slot_tokens, slot_weights = slot_tokens.reshape(1, -1), slot_weights.reshape(1, -1)
        inputs, cotangents, backs, returned = exchange(
            mesh, tokens, gate_weight, up_weight, down_weight, slot_tokens, slot_weights, out_grad)
        return finish(
            inputs, cotangents, backs, returned, out_grad, slot_tokens, slot_weights, gate_weight)

    split = P("dp", "expert")
    wide = P("expert", "dp", None)
    slot = P(None, "dp")
    return jax.shard_map(
        body, mesh=mesh,
        in_specs=(split, wide, wide, wide, slot, slot, split),
        out_specs=(split, wide, wide, wide),
        check_vma=False)
```

time: 35.2 us -> 28.3 us (0.80)
  local copies, waits for them, and re-layouts: 7.37 us -> 1.31 us
  Pallas kernels: 26.9 us -> 26.1 us
    unnamed x12 -> x6, local copies, waits for them, and re-layouts: 7.37 us -> 1.31 us
    pallas_call x1, Pallas kernels: 23.9 us -> 23.1 us  [exchange(): pl.pallas_call(functools.partial(exchange_kernel, rows, experts), out_sha...]
where the time goes in v2:
time: 28.3 us; the launch traced here: 28.1 us
  Pallas kernels  26.1 us (92%)
  local copies, waits for them, and re-layouts  1.31 us (5%)
  between operations  0.66 us (2%)
    pallas_call x1, Pallas kernels, exchange(): pl.pallas_call(functools.partial(exchange_kernel, rows, experts), out_sha...  23.1 us
    pallas_call x1, Pallas kernels, finish(): pl.pallas_call(finish_kernel, out_shape=(jax.ShapeDtypeStruct(grads.shape...  3 us
    unnamed x6, local copies, waits for them, and re-layouts  1.31 us

profile of v2, /device:TPU:0, one launch (start us, length us, event | category | flops | bytes accessed | tf_op | source)
XLA Modules:
  0.0 28.1 jit_solution(4008742462991128725)
XLA Ops:
  0.6 0.0 copy-start.1
  0.6 0.6 %copy-done.1 = s32[4,1]{0,1:T(1,128)S(1)} copy-done((s32[4,1]{0,1:T(1,128)S(1)}, s32[4,1]{0,1:T(1,128)}, u32[]{:S(2)}) %copy-start.1) | copy-done | bytes 40
  1.3 0.0 copy-start.2
  1.3 0.7 %copy-done.2 = f32[4,1]{0,1:T(1,128)S(1)} copy-done((f32[4,1]{0,1:T(1,128)S(1)}, f32[4,1]{0,1:T(1,128)}, u32[]{:S(2)}) %copy-start.2) | copy-done | bytes 40
  1.9 0.0 copy-start
  1.9 23.1 %exchange.1 = (bf16[8,3584]{1,0:T(8,128)(2,1)S(1)}, bf16[8,3584]{1,0:T(8,128)(2,1)S(1)}, bf16[3,8,192]{2,1,0:T(8,128)(2,1)S(1)}, f32[4,8,128]{2,1,0:T(8,128)S(1)}) custom-call(bf16[128,896]{1,0:T(8,128)(2,1)} %tokens.1, bf16[128,896]{1,0:T(8,128)(2,1)} %grads.3, bf16[1,192,3584]{2,1,0:T(8,128)(2,1)} %gate_w.1, bf16[1,192,3584]{2,1,0:T(8,128)(2,1)} %up_w.1, ...), custom_call_target="tpu_custom_call" | custom-call | tf_op jit(solution)/shard_map/exchange/pallas_call | solution.py:180
  25.1 0.0 copy-done
  25.1 3.0 %finish.1 = (bf16[128,896]{1,0:T(8,128)(2,1)}, bf16[1,192,3584]{2,1,0:T(8,128)(2,1)}, bf16[1,192,3584]{2,1,0:T(8,128)(2,1)}, bf16[1,192,3584]{2,1,0:T(8,128)(2,1)}) custom-call(bf16[8,3584]{1,0:T(8,128)(2,1)S(1)} %get-tuple-element.8.inputs, bf16[8,3584]{1,0:T(8,128)(2,1)S(1)} %get-tuple-element.9.cotangents, ...), custom_call_target="tpu_custom_call" | custom-call | tf_op jit(solution)/shard_map/finish/pallas_call | solution.py:253
Async XLA Ops:
  0.6 0.7 %copy-start.1 = (s32[4,1]{0,1:T(1,128)S(1)}, s32[4,1]{0,1:T(1,128)}, u32[]{:S(2)}) copy-start(s32[4,1]{0,1:T(1,128)} %param.11) | copy-start | bytes 52
  1.3 0.7 %copy-start.2 = (f32[4,1]{0,1:T(1,128)S(1)}, f32[4,1]{0,1:T(1,128)}, u32[]{:S(2)}) copy-start(f32[4,1]{0,1:T(1,128)} %param.12) | copy-start | bytes 52
  1.9 23.1 %copy-start = (bf16[128,896]{1,0:T(8,128)(2,1)S(1)}, bf16[128,896]{1,0:T(8,128)(2,1)}, u32[]{:S(2)}) copy-start(bf16[128,896]{1,0:T(8,128)(2,1)} %grads.3) | copy-start | bytes 688132
